TPU v7x, 256 devices: a whole 4x4x8 slice. The times are simulated.
256 devices in a mesh: rows: 32 (over x, z_lo, core), ch: 8 (over y, z_hi).
Axes of the slice: x: 4, y: 4, z: 8 (z_hi: 2, z_lo: 4; z = z_hi * 4 + z_lo), core: 2. Of those that a mesh axis runs over, the one named last changes fastest.
Arguments:
- features: bfloat16 [1536, 32768], P('ch', 'rows'), may hold values from -6 to 6
- cotangent: bfloat16 [1536, 32768], P('ch', 'rows'), may hold values from -6 to 6
- blocks: bfloat16 [256, 128, 128], P('rows'), may hold values from -0.5 to 0.5
- twiddles: float32 [2, 8, 32768], P(None, None, 'rows'), may hold values from -0.75 to 0.85, as said below
- channel_weight: bfloat16 [1536, 1536], P('ch'), may hold values from -0.15625 to 0.15625
Outputs:
- grad_features: bfloat16 [1536, 32768], P('ch', 'rows')
- grad_weight: float32 [1536, 1536], P('ch', 'rows')
Inputs may be any that keep to these rules, and one draw needn't show every extreme that they name: twiddles[0] lies in 0.55 to 0.85; twiddles[1] has magnitude 0.35 to 0.75 with either sign.
All inputs are finite; a program needn't handle non-finite values.
Results may differ from a plain program's by a relative error of at most 0.04.
Values may be sent and summed in bfloat16 or wider, within the bound.
A program may use at most 64 MiB of HBM per device.

v0:
```python
import jax
import jax.numpy as jnp
from jax import lax
from jax.sharding import PartitionSpec as P


def partner(value, axis, apart):
    mask = 2**apart
    pairs = [(source, source ^ mask) for source in range(lax.axis_size(axis))]
    return lax.ppermute(value, axis, pairs)


def flip_axis(h, dist, axis):
    n = h.shape[axis]
    shape = h.shape[:axis] + (n // (2 * dist), 2, dist) + h.shape[axis + 1 :]
    return jnp.flip(h.reshape(shape), axis + 1).reshape(h.shape)


def combine(own, other, mine, theirs):
    return (own * mine.astype(jnp.float32) + other * theirs.astype(jnp.float32)).astype(
        jnp.bfloat16
    )


def gelu_value(v):
    return 0.5 * v * (1.0 + lax.erf(v * 0.7071067811865476))


def gelu_slope(v):
    return (
        0.5 * (1.0 + lax.erf(v * 0.7071067811865476))
        + v * jnp.exp(-0.5 * v * v) * 0.3989422804014327
    )


def per_device(features, cotangent, blocks, twiddles, channel_weight):
    chan_local, tok_local = features.shape
    width = blocks.shape[1]
    count = blocks.shape[0]
    levels = twiddles.shape[1]
    shards = lax.axis_size("rows")
    cross = shards.bit_length() - 1
    local_levels = levels - cross
    mixed = (
        jnp.einsum(
            "brs,cbs->cbr",
            blocks,
            features.reshape(chan_local, count, width),
            preferred_element_type=jnp.float32,
        )
        .astype(jnp.bfloat16)
        .reshape(chan_local, tok_local)
    )
    for level in range(local_levels):
        mixed = combine(
            twiddles[0, level][None, :],
            twiddles[1, level][None, :],
            mixed,
            flip_axis(mixed, width * 2**level, 1),
        )
    for step in range(cross):
        level = local_levels + step
        theirs = partner(mixed, "rows", step)
        mixed = combine(twiddles[0, level][None, :], twiddles[1, level][None, :], mixed, theirs)
    mixed_wide = mixed.astype(jnp.float32)
    activated = gelu_value(mixed_wide).astype(jnp.bfloat16)
    piece = lax.all_gather(cotangent, "ch", axis=0, tiled=True)
    grad_acc = jnp.dot(channel_weight, piece, preferred_element_type=jnp.float32)
    update = lax.dot_general(
        activated, piece, (((1,), (1,)), ((), ())), preferred_element_type=jnp.float32
    )
    weight_acc = update
    grad_acc, weight_acc = (grad_acc, weight_acc)
    scale = 1.0 / (tok_local * shards) ** 0.5
    grad_weight = lax.psum_scatter(weight_acc * scale, "rows", scatter_dimension=1, tiled=True)
    back = (grad_acc * gelu_slope(mixed_wide)).astype(jnp.bfloat16)
    for step in reversed(range(cross)):
        level = local_levels + step
        sent = (twiddles[1, level][None, :] * back.astype(jnp.float32)).astype(jnp.bfloat16)
        theirs = partner(sent, "rows", step)
        back = (
            twiddles[0, level][None, :] * back.astype(jnp.float32) + theirs.astype(jnp.float32)
        ).astype(jnp.bfloat16)
    for level in reversed(range(local_levels)):
        sent = (twiddles[1, level][None, :] * back.astype(jnp.float32)).astype(jnp.bfloat16)
        back = (
            twiddles[0, level][None, :] * back.astype(jnp.float32)
            + flip_axis(sent, width * 2**level, 1).astype(jnp.float32)
        ).astype(jnp.bfloat16)
    grad_features = (
        jnp.einsum(
            "brs,cbr->cbs",
            blocks,
            back.reshape(chan_local, count, width),
            preferred_element_type=jnp.float32,
        )
        .astype(jnp.bfloat16)
        .reshape(chan_local, tok_local)
    )
    return (grad_features, grad_weight)


def solution(mesh):
    return jax.shard_map(
        per_device,
        mesh=mesh,
        in_specs=(
            P("ch", "rows"),
            P("ch", "rows"),
            P("rows", None, None),
            P(None, None, "rows"),
            P("ch", None),
        ),
        out_specs=(P("ch", "rows"), P("ch", "rows")),
        check_vma=False,
    )
```

profile of v0, /device:TPU:1, one launch (start us, length us, event | category | flops | bytes accessed | tf_op | source)
XLA Modules:
  0.0 300.6 jit_solution(1301715723498815556)
XLA Ops:
  7.2 0.7 all-gather.2.cloned.1.call-update
  8.0 1.4 convolution_convert_fusion.1
  9.3 0.1 fusion.40
  9.5 0.5 copy.12
  10.0 1.4 reshape.176
  11.4 1.3 reshape.179
  12.6 0.4 copy.13
  13.0 2.8 rev.21
  15.9 0.5 reshape.177
  16.4 1.3 reshape.180
  17.8 1.2 add_convert_fusion.10
  18.9 4.7 %rev.22 = bf16[192,2,2,256]{3,2,1,0:T(2,128)(2,1)S(1)} reverse(bf16[192,2,2,256]{3,2,1,0:T(2,128)(2,1)} %add_convert_fusion.10), dimensions={2} | reverse | bytes 786432 | tf_op jit(solution)/shard_map/jit(_flip)/rev | solution.py:16
  23.7 1.4 reshape.181
  25.1 0.2 reshape.178
  25.3 0.2 reshape.175
  25.5 3.2 %add_convert_fusion.7 = bf16[192,1,2,512]{3,2,0,1:T(2,128)(2,1)} fusion(f32[192,1,2,512]{3,2,0,1:T(2,128)} %reshape.181, f32[192,1,2,512]{3,2,0,1:T(2,128)} %reshape.180, f32[192,1,2,512]{3,2,0,1:T(2,128)} %reshape.179, f32[2,512]{1,0:T(2,128)S(1)} %mul.404, f32[2,512]{1,0:T(2,128)S(1)} %mul.400, f32[2,512]{1,0:T(2,128)S(1)} %mul.397, f32[2,512]{1,0:T(2,128)S(1)} %mul.395), kind=kLoop, calls=%fused_computation.65 | loop fusion | flops 1769472 | bytes 2768896 | tf_op jit(solution)/shard_map/convert_element_type | solution.py:20
  28.7 4.7 %rev.23 = bf16[192,1,2,512]{3,2,0,1:T(2,128)(2,1)S(1)} reverse(bf16[192,1,2,512]{3,2,0,1:T(2,128)(2,1)} %add_convert_fusion.7), dimensions={2} | reverse | bytes 786432 | tf_op jit(solution)/shard_map/jit(_flip)/rev | solution.py:16
  33.4 0.1 copy.22
  33.5 0.3 add_convert_fusion.6
  33.9 3.2 %collective-permute-start = (bf16[192,1024]{1,0:T(8,128)(2,1)S(1)}, bf16[192,1024]{1,0:T(8,128)(2,1)S(1)}, u32[]{:S(2)}, u32[]{:S(2)}) collective-permute-start(bf16[192,1024]{1,0:T(8,128)(2,1)S(1)} %add_convert_fusion.6), channel_id=1, source_target_pairs={{0,8},{8,0},{16,24},{24,16},{32,40},{40,32},{48,56},{56,48},{64,72... | collective-permute-start | bytes 1179656 | tf_op jit(solution)/shard_map/ppermute | solution.py:10
  37.1 1.3 collective-permute-done
  38.4 0.2 add_convert_fusion.5
  38.6 0.1 collective-permute-start.1
  38.7 10.4 %collective-permute-done.1 = bf16[192,1024]{1,0:T(8,128)(2,1)S(1)} collective-permute-done((bf16[192,1024]{1,0:T(8,128)(2,1)S(1)}, bf16[192,1024]{1,0:T(8,128)(2,1)S(1)}, u32[]{:S(2)}, u32[]{:S(2)}) %collective-permute-start.1) | collective-permute-done | bytes 393248 | tf_op jit(solution)/shard_map/ppermute | solution.py:10
  49.1 0.2 add_convert_fusion.4
  49.2 1.7 collective-permute-start.2
  51.0 51.8 %collective-permute-done.2 = bf16[192,1024]{1,0:T(8,128)(2,1)S(1)} collective-permute-done((bf16[192,1024]{1,0:T(8,128)(2,1)S(1)}, bf16[192,1024]{1,0:T(8,128)(2,1)S(1)}, u32[]{:S(2)}, u32[]{:S(2)}) %collective-permute-start.2) | collective-permute-done | bytes 393248 | tf_op jit(solution)/shard_map/ppermute | solution.py:10
  102.7 0.2 add_convert_fusion.3
  102.9 0.1 collective-permute-start.3
  103.0 9.4 %collective-permute-done.3 = bf16[192,1024]{1,0:T(8,128)(2,1)S(1)} collective-permute-done((bf16[192,1024]{1,0:T(8,128)(2,1)S(1)}, bf16[192,1024]{1,0:T(8,128)(2,1)S(1)}, u32[]{:S(2)}, u32[]{:S(2)}) %collective-permute-start.3) | collective-permute-done | bytes 393248 | tf_op jit(solution)/shard_map/ppermute | solution.py:10
  112.4 0.1 add_convert_fusion.2
  112.6 1.2 collective-permute-start.4
  113.8 9.0 %collective-permute-done.4 = bf16[192,1024]{1,0:T(8,128)(2,1)S(1)} collective-permute-done((bf16[192,1024]{1,0:T(8,128)(2,1)S(1)}, bf16[192,1024]{1,0:T(8,128)(2,1)S(1)}, u32[]{:S(2)}, u32[]{:S(2)}) %collective-permute-start.4) | collective-permute-done | bytes 393248 | tf_op jit(solution)/shard_map/ppermute | solution.py:10
  122.7 3.0 multiply_convert_fusion
  125.8 0.8 collective-permute-start.5
  126.6 8.5 %collective-permute-done.5 = bf16[192,1024]{1,0:T(8,128)(2,1)S(1)} collective-permute-done((bf16[192,1024]{1,0:T(8,128)(2,1)S(1)}, bf16[192,1024]{1,0:T(8,128)(2,1)S(1)}, u32[]{:S(2)}, u32[]{:S(2)}) %collective-permute-start.5) | collective-permute-done | bytes 393248 | tf_op jit(solution)/shard_map/ppermute | solution.py:10
  135.1 0.2 fusion.5
  135.3 0.1 collective-permute-start.6
  135.4 6.6 %collective-permute-done.6 = bf16[192,1024]{1,0:T(8,128)(2,1)S(1)} collective-permute-done((bf16[192,1024]{1,0:T(8,128)(2,1)S(1)}, bf16[192,1024]{1,0:T(8,128)(2,1)S(1)}, u32[]{:S(2)}, u32[]{:S(2)}) %collective-permute-start.6) | collective-permute-done | bytes 393248 | tf_op jit(solution)/shard_map/ppermute | solution.py:10
  142.0 0.2 fusion.8
  142.3 0.1 collective-permute-start.7
  142.4 2.3 convolution_multiply_fusion
  144.7 5.2 %collective-permute-done.7 = bf16[192,1024]{1,0:T(8,128)(2,1)S(1)} collective-permute-done((bf16[192,1024]{1,0:T(8,128)(2,1)S(1)}, bf16[192,1024]{1,0:T(8,128)(2,1)S(1)}, u32[]{:S(2)}, u32[]{:S(2)}) %collective-permute-start.7) | collective-permute-done | bytes 393248 | tf_op jit(solution)/shard_map/ppermute | solution.py:10
  149.9 0.2 fusion.11
  150.0 12.1 %collective-permute-start.8 = (bf16[192,1024]{1,0:T(8,128)(2,1)S(1)}, bf16[192,1024]{1,0:T(8,128)(2,1)S(1)}, u32[]{:S(2)}, u32[]{:S(2)}) collective-permute-start(bf16[192,1024]{1,0:T(8,128)(2,1)S(1)} %fusion.11), channel_id=1, source_target_pairs={{0,16},{8,24},{16,0},{24,8},{32,48},{40,56},{48,32},{56,40},{64,80... | collective-permute-start | bytes 1179656 | tf_op jit(solution)/shard_map/ppermute | solution.py:10
  162.1 8.3 %collective-permute-done.8 = bf16[192,1024]{1,0:T(8,128)(2,1)S(1)} collective-permute-done((bf16[192,1024]{1,0:T(8,128)(2,1)S(1)}, bf16[192,1024]{1,0:T(8,128)(2,1)S(1)}, u32[]{:S(2)}, u32[]{:S(2)}) %collective-permute-start.8) | collective-permute-done | bytes 393248 | tf_op jit(solution)/shard_map/ppermute | solution.py:10
  170.5 0.3 fusion.14
  170.7 3.1 %collective-permute-start.9 = (bf16[192,1024]{1,0:T(8,128)(2,1)S(1)}, bf16[192,1024]{1,0:T(8,128)(2,1)S(1)}, u32[]{:S(2)}, u32[]{:S(2)}) collective-permute-start(bf16[192,1024]{1,0:T(8,128)(2,1)S(1)} %get-tuple-element.10), channel_id=1, source_target_pairs={{0,8},{8,0},{16,24},{24,16},{32,40},{40,32},{48,56},{56,48},{64,72... | collective-permute-start | bytes 1179656 | tf_op jit(solution)/shard_map/ppermute | solution.py:10
  173.9 1.3 collective-permute-done.9
  175.2 0.2 fusion.17
  175.4 0.3 reshape.169
  175.7 2.9 rev.24
  178.6 0.1 copy.23
  178.7 0.2 fusion.20
  178.9 0.3 reshape.170
  179.2 2.9 rev.25
  182.1 0.2 reshape.184
  182.3 0.2 fusion.23
  182.5 0.3 reshape.171
  182.8 2.8 rev.26
  185.6 0.2 reshape.185
  185.8 0.3 fusion.2
  186.1 0.9 copy.36
  187.0 106.8 %reduce-scatter.2.cloned.1.call-done = f32[192,48]{0,1:T(8,128)} async-done(((f32[192,1536]{0,1:T(8,128)}), f32[192,48]{0,1:T(8,128)}) %reduce-scatter.2.cloned.1.call-update) | async-done | bytes 36880 | tf_op jit(solution)/shard_map/reduce_scatter | solution.py:75
  (22 shorter events, 0.3 us)
Async XLA Ops:
  7.2 115.6 %copy-start = (bf16[192,1536]{1,0:T(8,128)(2,1)S(1)}, bf16[192,1536]{1,0:T(8,128)(2,1)}, u32[]{:S(2)}) copy-start(bf16[192,1536]{1,0:T(8,128)(2,1)} %param.9) | copy-start | bytes 1769476
  7.2 115.6 %all-gather.2.cloned.1.call-start = ((), (), s32[]{:S(2)}) async-start(), calls=%async_computation.1 | async-start | bytes 3538944 | tf_op jit(solution)/shard_map/all_gather | solution.py:67
  7.9 285.9 %reduce-scatter.2.cloned.1.call-start = ((), (), s32[]{:S(2)}) async-start(), calls=%async_computation.2 | async-start | bytes 1622016 | tf_op jit(solution)/shard_map/reduce_scatter | solution.py:75
  11.4 6.3 %copy-start.3 = (f32[2,8,1024]{2,1,0:T(8,128)S(1)}, f32[2,8,1024]{2,1,0:T(8,128)}, u32[]{:S(2)}) copy-start(f32[2,8,1024]{2,1,0:T(8,128)} %param.8) | copy-start | bytes 196612
  12.6 5.1 %copy-start.1 = (f32[192,2,2,256]{3,2,1,0:T(2,128)S(1)}, f32[192,2,2,256]{3,2,1,0:T(2,128)}, u32[]{:S(2)}) copy-start(f32[192,2,2,256]{3,2,1,0:T(2,128)} %reshape.176) | copy-start | bytes 2359300
  33.9 4.6 %collective-permute-start = (bf16[192,1024]{1,0:T(8,128)(2,1)S(1)}, bf16[192,1024]{1,0:T(8,128)(2,1)S(1)}, u32[]{:S(2)}, u32[]{:S(2)}) collective-permute-start(bf16[192,1024]{1,0:T(8,128)(2,1)S(1)} %add_convert_fusion.6), channel_id=1, source_target_pairs={{0,8},{8,0},{16,24},{24,16},{32,40},{40,32},{48,56},{56,48},{64,72... | collective-permute-start | bytes 1179656 | tf_op jit(solution)/shard_map/ppermute | solution.py:10
  38.6 10.5 %collective-permute-start.1 = (bf16[192,1024]{1,0:T(8,128)(2,1)S(1)}, bf16[192,1024]{1,0:T(8,128)(2,1)S(1)}, u32[]{:S(2)}, u32[]{:S(2)}) collective-permute-start(bf16[192,1024]{1,0:T(8,128)(2,1)S(1)} %add_convert_fusion.5), channel_id=1, source_target_pairs={{0,16},{8,24},{16,0},{24,8},{32,48},{40,56},{48,32},{56,40},{64,80... | collective-permute-start | bytes 1179656 | tf_op jit(solution)/shard_map/ppermute | solution.py:10
  49.2 53.5 %collective-permute-start.2 = (bf16[192,1024]{1,0:T(8,128)(2,1)S(1)}, bf16[192,1024]{1,0:T(8,128)(2,1)S(1)}, u32[]{:S(2)}, u32[]{:S(2)}) collective-permute-start(bf16[192,1024]{1,0:T(8,128)(2,1)S(1)} %add_convert_fusion.4), channel_id=1, source_target_pairs={{0,32},{8,40},{16,48},{24,56},{32,0},{40,8},{48,16},{56,24},{64,96... | collective-permute-start | bytes 1179656 | tf_op jit(solution)/shard_map/ppermute | solution.py:10
  102.9 9.6 %collective-permute-start.3 = (bf16[192,1024]{1,0:T(8,128)(2,1)S(1)}, bf16[192,1024]{1,0:T(8,128)(2,1)S(1)}, u32[]{:S(2)}, u32[]{:S(2)}) collective-permute-start(bf16[192,1024]{1,0:T(8,128)(2,1)S(1)} %add_convert_fusion.3), channel_id=1, source_target_pairs={{0,64},{8,72},{16,80},{24,88},{32,96},{40,104},{48,112},{56,120},{... | collective-permute-start | bytes 1179656 | tf_op jit(solution)/shard_map/ppermute | solution.py:10
  112.6 10.1 %collective-permute-start.4 = (bf16[192,1024]{1,0:T(8,128)(2,1)S(1)}, bf16[192,1024]{1,0:T(8,128)(2,1)S(1)}, u32[]{:S(2)}, u32[]{:S(2)}) collective-permute-start(bf16[192,1024]{1,0:T(8,128)(2,1)S(1)} %add_convert_fusion.2), channel_id=1, source_target_pairs={{0,128},{8,136},{16,144},{24,152},{32,160},{40,168},{48,176},{56,1... | collective-permute-start | bytes 1179656 | tf_op jit(solution)/shard_map/ppermute | solution.py:10
  125.7 16.6 %copy-start.4 = (bf16[1536,1024]{1,0:T(8,128)(2,1)S(1)}, bf16[1536,1024]{1,0:T(8,128)(2,1)}, u32[]{:S(2)}) copy-start(bf16[1536,1024]{1,0:T(8,128)(2,1)} %all-gather.2.cloned.1.call-done) | copy-start | bytes 9437188
  125.8 9.4 %collective-permute-start.5 = (bf16[192,1024]{1,0:T(8,128)(2,1)S(1)}, bf16[192,1024]{1,0:T(8,128)(2,1)S(1)}, u32[]{:S(2)}, u32[]{:S(2)}) collective-permute-start(bf16[192,1024]{1,0:T(8,128)(2,1)S(1)} %get-tuple-element.34), channel_id=1, source_target_pairs={{0,128},{8,136},{16,144},{24,152},{32,160},{40,168},{48,176},{56,1... | collective-permute-start | bytes 1179656 | tf_op jit(solution)/shard_map/ppermute | solution.py:10
  135.3 6.7 %collective-permute-start.6 = (bf16[192,1024]{1,0:T(8,128)(2,1)S(1)}, bf16[192,1024]{1,0:T(8,128)(2,1)S(1)}, u32[]{:S(2)}, u32[]{:S(2)}) collective-permute-start(bf16[192,1024]{1,0:T(8,128)(2,1)S(1)} %get-tuple-element.14), channel_id=1, source_target_pairs={{0,64},{8,72},{16,80},{24,88},{32,96},{40,104},{48,112},{56,120},{... | collective-permute-start | bytes 1179656 | tf_op jit(solution)/shard_map/ppermute | solution.py:10
  142.3 7.6 %collective-permute-start.7 = (bf16[192,1024]{1,0:T(8,128)(2,1)S(1)}, bf16[192,1024]{1,0:T(8,128)(2,1)S(1)}, u32[]{:S(2)}, u32[]{:S(2)}) collective-permute-start(bf16[192,1024]{1,0:T(8,128)(2,1)S(1)} %get-tuple-element.12), channel_id=1, source_target_pairs={{0,32},{8,40},{16,48},{24,56},{32,0},{40,8},{48,16},{56,24},{64,96... | collective-permute-start | bytes 1179656 | tf_op jit(solution)/shard_map/ppermute | solution.py:10
  150.0 20.5 %collective-permute-start.8 = (bf16[192,1024]{1,0:T(8,128)(2,1)S(1)}, bf16[192,1024]{1,0:T(8,128)(2,1)S(1)}, u32[]{:S(2)}, u32[]{:S(2)}) collective-permute-start(bf16[192,1024]{1,0:T(8,128)(2,1)S(1)} %fusion.11), channel_id=1, source_target_pairs={{0,16},{8,24},{16,0},{24,8},{32,48},{40,56},{48,32},{56,40},{64,80... | collective-permute-start | bytes 1179656 | tf_op jit(solution)/shard_map/ppermute | solution.py:10
  170.7 4.5 %collective-permute-start.9 = (bf16[192,1024]{1,0:T(8,128)(2,1)S(1)}, bf16[192,1024]{1,0:T(8,128)(2,1)S(1)}, u32[]{:S(2)}, u32[]{:S(2)}) collective-permute-start(bf16[192,1024]{1,0:T(8,128)(2,1)S(1)} %get-tuple-element.10), channel_id=1, source_target_pairs={{0,8},{8,0},{16,24},{24,16},{32,40},{40,32},{48,56},{56,48},{64,72... | collective-permute-start | bytes 1179656 | tf_op jit(solution)/shard_map/ppermute | solution.py:10
  182.1 3.7 %copy-start.2 = (bf16[8,128,128]{2,1,0:T(8,128)(2,1)S(1)}, bf16[8,128,128]{2,1,0:T(8,128)(2,1)}, u32[]{:S(2)}) copy-start(bf16[8,128,128]{2,1,0:T(8,128)(2,1)} %param.7) | copy-start | bytes 786436
Sparse Core Ops, SparseCore 0:
  10.6 98.0 all-gather.1
  144.8 148.9 reduce-scatter.1
where the time goes:
time: 305 us; the launch traced here: 301 us
  waiting for transfers between devices  219 us (72%)
  local copies, waits for them, and re-layouts  30.4 us (10%)
  starting transfers between devices  22.7 us (7%)
  between operations  14.4 us (5%)
  matrix products  6.93 us (2%)
  other arithmetic  6.79 us (2%)
    ppermute x10, waiting for transfers between devices, partner(): return lax.ppermute(value, axis, pairs)  112 us
    reduce_scatter x1, waiting for transfers between devices, per_device(): lax.psum_scatter(weight_acc * scale, 'rows', scatter_dimension=1, tiled=T...  107 us
    ppermute x10, starting transfers between devices, partner(): return lax.ppermute(value, axis, pairs)  22.6 us
    rev x6, local copies, waits for them, and re-layouts, flip_axis(): return jnp.flip(h.reshape(shape), axis + 1).reshape(h.shape)  20.9 us
  transfers between devices with their start and end apart: 12, of which 11 were waited for; matrix products, arithmetic and copies ran while one was open for 14% of the time, Pallas kernels for 0%

commit v1 on v0

v1 whole, which is shorter than its diff:
```python
import jax
import jax.numpy as jnp
from jax import lax
from jax.experimental import pallas as pl
from jax.experimental.pallas import tpu as pltpu
from jax.sharding import PartitionSpec as P

MESH = pl.DeviceIdType.MESH
F32 = jnp.float32
BF16 = jnp.bfloat16

NX, NZ, NC, NY = 4, 4, 2, 4
ROWS = NX * NZ * NC
CHS = 2 * NY
BLK = 128
LOCAL = 3
LEVELS = 8
CHUNKS = 4


def gelu_parts(v):
    half = 0.5 * (1.0 + lax.erf(v * 0.7071067811865476))
    act = v * half
    slope = half + v * jnp.exp(-0.5 * v * v) * 0.3989422804014327
    return act, slope


def flip(v, dist):
    n = v.shape[0]
    h = v.reshape((n // (2 * dist), 2, dist) + v.shape[1:])
    h = jnp.concatenate([h[:, 1:], h[:, :1]], axis=1)
    return h.reshape(v.shape)


def body(
    feat_hbm, cot_hbm, blocks_hbm, tw_hbm, w_hbm,
    gf_ref, gw_ref,
    feat, blocks, tw, w, cot,
    twst, twz, twall, twb, twl, m0, gacc, act,
    s1, r1, s2, r2, s3, r3, s4, r4,
    gst, rc, p1, rx, p2, rz, fin,
    loc_sem, a2a_send, a2a_recv, tw_send, tw_recv,
    cz_send, cz_recv, cy_send, cy_recv, g_send, g_recv,
):
    row = lax.axis_index("rows")
    col = lax.axis_index("ch")
    x, zl, c = row // (NZ * NC), (row // NC) % NZ, row % NC
    y = col // 2
    zc = row % (NZ * NC)
    up = {"ch": ((y + 1) % NY) * 2 + col % 2}
    down = {"ch": ((y + NY - 1) % NY) * 2 + col % 2}
    across = {"ch": y * 2 + (1 - col % 2)}
    tok = feat.shape[1]
    chan = feat.shape[0]
    quarter = chan // NX

    loads = [
        pltpu.make_async_copy(feat_hbm, feat, loc_sem.at[0]),
        pltpu.make_async_copy(blocks_hbm, blocks, loc_sem.at[1]),
        pltpu.make_async_copy(tw_hbm, tw, loc_sem.at[2]),
        pltpu.make_async_copy(cot_hbm, cot.at[col], loc_sem.at[3]),
        pltpu.make_async_copy(w_hbm, w, loc_sem.at[4]),
    ]
    for load in loads:
        load.start()

    bar = pltpu.get_barrier_semaphore()

    def greet(i, carry):
        pl.semaphore_signal(bar, inc=1, device_id={"rows": (row + i) % ROWS}, device_id_type=MESH)
        return carry

    lax.fori_loop(1, ROWS, greet, 0)
    for peer in (up, down, across):
        pl.semaphore_signal(bar, inc=1, device_id=peer, device_id_type=MESH)

    loads[2].wait()
    for b in range(NZ * NC):
        part = tw[:, :, b * BLK : (b + 1) * BLK]
        twst[b] = part.reshape(2 * LEVELS, BLK).astype(BF16)
        for j in range(LOCAL):
            for s in range(2):
                twl[s, j, b] = jnp.broadcast_to(tw[s, j : j + 1, b * BLK : (b + 1) * BLK], (8, BLK))

    pl.semaphore_wait(bar, ROWS - 1 + 3)

    def twz_send(i, carry):
        other = (zc + i) % (NZ * NC)
        pltpu.make_async_remote_copy(
            src_ref=twst.at[other], dst_ref=twz.at[zc],
            send_sem=tw_send.at[0], recv_sem=tw_recv.at[0],
            device_id={"rows": x * (NZ * NC) + other}, device_id_type=MESH,
        ).start()
        return carry

    lax.fori_loop(1, NZ * NC, twz_send, 0)
    pltpu.make_async_copy(twst.at[zc], twz.at[zc], tw_recv.at[0]).start()

    loads[0].wait()
    loads[1].wait()
    for g in range(NZ * NC):
        m0[g] = lax.dot_general(
            feat[:, g * BLK : (g + 1) * BLK], blocks[g], (((1,), (1,)), ((), ())),
            preferred_element_type=F32,
        )

    def local_fwd(t, carry):
        rows8 = pl.ds(pl.multiple_of(t * 16, 16), 16)
        v = m0[:, rows8, :].reshape(NZ * NC, 2, 8, BLK)
        for j in range(LOCAL):
            v = v * twl[0, j][:, None] + flip(v, 2**j) * twl[1, j][:, None]
        v = v.reshape(NZ * NC, 16, BLK).astype(BF16)
        per = quarter // 16
        s1[t // per, :, pl.ds(pl.multiple_of((t % per) * 16, 16), 16), :] = v
        return carry

    lax.fori_loop(0, chan // 16, local_fwd, 0)

    def exchange(step, src, dst):
        def one(i, carry):
            other = (row + i) % ROWS
            pltpu.make_async_remote_copy(
                src_ref=src.at[other // 8, other % 8], dst_ref=dst.at[row // 8, row % 8],
                send_sem=a2a_send.at[step], recv_sem=a2a_recv.at[step],
                device_id={"rows": other}, device_id_type=MESH,
            ).start()
            return carry

        lax.fori_loop(1, ROWS, one, 0)
        pltpu.make_async_copy(
            src.at[row // 8, row % 8], dst.at[row // 8, row % 8], a2a_recv.at[step]
        ).start()

    def arrived(step, dst):
        pltpu.make_async_copy(dst, dst, a2a_recv.at[step]).wait()

    exchange(0, s1, r1)

    size = chan // CHUNKS

    def cz(k):
        part = pl.ds(k * size, size)
        return pltpu.make_async_remote_copy(
            src_ref=cot.at[col, part], dst_ref=cot.at[col, part],
            send_sem=cz_send.at[k], recv_sem=cz_recv.at[k],
            device_id=across, device_id_type=MESH,
        )

    def cy(way, owner, k, which):
        part = pl.ds(k * size, size)
        return pltpu.make_async_remote_copy(
            src_ref=cot.at[owner, part], dst_ref=cot.at[owner, part],
            send_sem=cy_send.at[which, k, way], recv_sem=cy_recv.at[which, k, way],
            device_id=(up, down)[way], device_id_type=MESH,
        )

    loads[3].wait()
    own_y = [cy(way, col, k, 0) for k in range(CHUNKS) for way in range(2)]
    own_z = [cz(k) for k in range(CHUNKS)]
    for copy in own_y:
        copy.start()
    for copy in own_z:
        copy.start()

    pltpu.make_async_copy(twz, twz, tw_recv.at[0]).wait()

    def twx_send(i, carry):
        other = (x + i) % NX
        pltpu.make_async_remote_copy(
            src_ref=twz, dst_ref=twall.at[x],
            send_sem=tw_send.at[1], recv_sem=tw_recv.at[1],
            device_id={"rows": other * (NZ * NC) + zc}, device_id_type=MESH,
        ).start()
        return carry

    lax.fori_loop(1, NX, twx_send, 0)
    pltpu.make_async_copy(twz, twall.at[x], tw_recv.at[1]).start()
    pltpu.make_async_copy(twall, twall, tw_recv.at[1]).wait()

    def spread(r, carry):
        t = twall[r // 8, r % 8].astype(F32)
        for j in range(LEVELS - LOCAL):
            for s in range(2):
                at = s * LEVELS + LOCAL + j
                twb[s, j, r] = jnp.broadcast_to(t[at : at + 1, :], (8, BLK))
        return carry

    lax.fori_loop(0, ROWS, spread, 0)

    def relay(which, base):
        sent = []
        for k in range(CHUNKS):
            way = 0 if k < CHUNKS // 2 else 1
            owner = ((y + NY - 1) % NY if way == 0 else (y + 1) % NY) * 2 + base
            cy(way, owner, k, which).wait_recv()
            copy = cy(way, owner, k, which + 1)
            copy.start()
            sent.append(copy)
        return sent

    relays = relay(0, col % 2)

    arrived(0, r1)

    def cross_fwd(t, carry):
        part = pl.ds(pl.multiple_of(t * 16, 16), 16)
        v = r1[:, :, part, :].astype(F32).reshape(ROWS, 2, 8, BLK)
        for j in range(LEVELS - LOCAL):
            v = v * twb[0, j][:, None] + flip(v, 2**j) * twb[1, j][:, None]
        s2[:, :, part, :] = v.reshape(NX, NZ * NC, 16, BLK).astype(BF16)
        return carry

    lax.fori_loop(0, quarter // 16, cross_fwd, 0)
    exchange(1, s2, r2)

    far = col - col % 2 + (1 - col % 2)
    far_y = []
    for k in range(CHUNKS):
        own_z[k].wait_recv()
        for way in range(2):
            copy = cy(way, far, k, 2)
            copy.start()
            far_y.append(copy)
    relays += relay(2, 1 - col % 2)

    for which in (0, 2):
        for k in range(CHUNKS):
            way = 1 if k < CHUNKS // 2 else 0
            cy(way, col, k, which).wait_recv()
    for which in (1, 3):
        for k in range(CHUNKS):
            way = 0 if k < CHUNKS // 2 else 1
            cy(way, col, k, which).wait_recv()

    loads[4].wait()

    def project(n, carry):
        part = pl.ds(pl.multiple_of(n * 256, 256), 256)
        piece = cot[:, :, part].reshape(CHS * chan, 256)
        gacc[:, part] = jnp.dot(w[...], piece, preferred_element_type=F32)
        return carry

    lax.fori_loop(0, tok // 256, project, 0)

    arrived(1, r2)

    def middle(q, carry):
        part = pl.ds(pl.multiple_of(q * quarter, 16), quarter)
        for b in range(NZ * NC):
            lanes = slice(b * BLK, (b + 1) * BLK)
            a, s = gelu_parts(r2[q, b].astype(F32))
            act[part, lanes] = a.astype(BF16)
            s3[q, b] = (gacc[part, lanes] * s).astype(BF16)
        return carry

    lax.fori_loop(0, NX, middle, 0)
    exchange(2, s3, r3)

    def weight(h, carry):
        g = lax.dot_general(
            cot[h], act[...], (((1,), (1,)), ((), ())), preferred_element_type=F32
        ).astype(BF16)
        for i in range(4):
            gst[i % 2, h // 2, (h % 2) * 2 + i // 2] = g[i * 48 : (i + 1) * 48]
        return carry

    lax.fori_loop(0, CHS, weight, 0)
    g_core = pltpu.make_async_remote_copy(
        src_ref=gst.at[1 - c], dst_ref=rc, send_sem=g_send.at[0], recv_sem=g_recv.at[0],
        device_id={"rows": row + 1 - 2 * c}, device_id_type=MESH,
    )
    g_core.start()
    g_core.wait_recv()
    for i in range(NX):
        p1[i] = (gst[c, i].astype(F32) + rc[i].astype(F32)).astype(BF16)

    def gx(i, carry):
        other = (x + i) % NX
        pltpu.make_async_remote_copy(
            src_ref=p1.at[other], dst_ref=rx.at[x], send_sem=g_send.at[1], recv_sem=g_recv.at[1],
            device_id={"rows": other * (NZ * NC) + zc}, device_id_type=MESH,
        ).start()
        return carry

    lax.fori_loop(1, NX, gx, 0)
    pltpu.make_async_copy(p1.at[x], rx.at[x], g_recv.at[1]).start()

    arrived(2, r3)

    def cross_bwd(t, carry):
        part = pl.ds(pl.multiple_of(t * 16, 16), 16)
        v = r3[:, :, part, :].astype(F32).reshape(ROWS, 2, 8, BLK)
        for j in reversed(range(LEVELS - LOCAL)):
            v = v * twb[0, j][:, None] + flip(v * twb[1, j][:, None], 2**j)
        s4[:, :, part, :] = v.reshape(NX, NZ * NC, 16, BLK).astype(BF16)
        return carry

    lax.fori_loop(0, quarter // 16, cross_bwd, 0)
    exchange(3, s4, r4)

    pltpu.make_async_copy(rx, rx, g_recv.at[1]).wait()
    for i in range(NZ):
        total = rx[0, i].astype(F32)
        for j in range(1, NX):
            total = total + rx[j, i].astype(F32)
        p2[i] = total.astype(BF16)

    def gz(i, carry):
        other = (zl + i) % NZ
        pltpu.make_async_remote_copy(
            src_ref=p2.at[other], dst_ref=rz.at[zl], send_sem=g_send.at[2], recv_sem=g_recv.at[2],
            device_id={"rows": x * (NZ * NC) + other * NC + c}, device_id_type=MESH,
        ).start()
        return carry

    lax.fori_loop(1, NZ, gz, 0)
    pltpu.make_async_copy(p2.at[zl], rz.at[zl], g_recv.at[2]).start()

    arrived(3, r4)

    def local_bwd(t, carry):
        per = quarter // 16
        v = r4[t // per, :, pl.ds(pl.multiple_of((t % per) * 16, 16), 16), :]
        v = v.astype(F32).reshape(NZ * NC, 2, 8, BLK)
        for j in reversed(range(LOCAL)):
            v = v * twl[0, j][:, None] + flip(v * twl[1, j][:, None], 2**j)
        v = v.reshape(NZ * NC, 16, BLK).astype(BF16)
        rows8 = pl.ds(pl.multiple_of(t * 16, 16), 16)
        for g in range(NZ * NC):
            feat[rows8, g * BLK : (g + 1) * BLK] = v[g]
        return carry

    lax.fori_loop(0, chan // 16, local_bwd, 0)
    for g in range(NZ * NC):
        lanes = slice(g * BLK, (g + 1) * BLK)
        gf_ref[:, lanes] = jnp.dot(
            feat[:, lanes], blocks[g], preferred_element_type=F32
        ).astype(BF16)

    pltpu.make_async_copy(rz, rz, g_recv.at[2]).wait()
    total = rz[0].astype(F32)
    for j in range(1, NZ):
        total = total + rz[j].astype(F32)
    fin[...] = jnp.zeros_like(fin)
    fin[:48, :chan] = total * (1.0 / (tok * ROWS) ** 0.5)
    gw_ref[...] = jnp.transpose(fin[...])[:chan, :48]

    for step, src in enumerate((s1, s2, s3, s4)):
        for part in (src.at[0:3], src.at[3, 0:7]):
            pltpu.make_async_copy(part, part, a2a_send.at[step]).wait()
    pltpu.make_async_copy(twst.at[0:7], twst.at[0:7], tw_send.at[0]).wait()
    pltpu.make_async_copy(twall.at[0:3], twall.at[0:3], tw_send.at[1]).wait()
    for copy in own_y + own_z + far_y + relays:
        copy.wait_send()
    g_core.wait_send()
    pltpu.make_async_copy(p1.at[0:3], p1.at[0:3], g_send.at[1]).wait()
    pltpu.make_async_copy(p2.at[0:3], p2.at[0:3], g_send.at[2]).wait()


def per_device(features, cotangent, blocks, twiddles, channel_weight):
    chan, tok = features.shape
    quarter = chan // NX
    nb = NZ * NC
    wide = channel_weight.shape[1]
    piece = (NX, nb, quarter, BLK)
    vm = pltpu.VMEM
    dma = pltpu.SemaphoreType.DMA
    scratch = [
        vm((chan, tok), BF16), vm(blocks.shape, BF16), vm(twiddles.shape, F32),
        vm(channel_weight.shape, BF16), vm((CHS, chan, tok), BF16),
        vm((nb, 2 * LEVELS, BLK), BF16), vm((nb, 2 * LEVELS, BLK), BF16),
        vm((NX, nb, 2 * LEVELS, BLK), BF16),
        vm((2, LEVELS - LOCAL, ROWS, 8, BLK), F32), vm((2, LOCAL, nb, 8, BLK), F32),
        vm((nb, chan, BLK), F32), vm((chan, tok), F32), vm((chan, tok), BF16),
        *[vm(piece, BF16)] * 8,
        vm((2, NX, NZ, 48, chan), BF16), vm((NX, NZ, 48, chan), BF16),
        vm((NX, NZ, 48, chan), BF16), vm((NX, NZ, 48, chan), BF16),
        vm((NZ, 48, chan), BF16), vm((NZ, 48, chan), BF16), vm((128, 256), F32),
        dma((5,)), dma((4,)), dma((4,)), dma((2,)), dma((2,)),
        dma((CHUNKS,)), dma((CHUNKS,)), dma((4, CHUNKS, 2)), dma((4, CHUNKS, 2)),
        dma((3,)), dma((3,)),
    ]
    return pl.pallas_call(
        body,
        out_shape=(
            jax.ShapeDtypeStruct((chan, tok), BF16),
            jax.ShapeDtypeStruct((chan, wide // ROWS), F32),
        ),
        in_specs=[pl.BlockSpec(memory_space=pl.ANY)] * 5,
        out_specs=(pl.BlockSpec(memory_space=pltpu.VMEM),) * 2,
        scratch_shapes=scratch,
        name="mixer",
        compiler_params=pltpu.CompilerParams(
            collective_id=0, has_side_effects=True, vmem_limit_bytes=48 << 20
        ),
    )(features, cotangent, blocks, twiddles, channel_weight)


def solution(mesh):
    return jax.shard_map(
        per_device,
        mesh=mesh,
        in_specs=(
            P("ch", "rows"),
            P("ch", "rows"),
            P("rows", None, None),
            P(None, None, "rows"),
            P("ch", None),
        ),
        out_specs=(P("ch", "rows"), P("ch", "rows")),
        check_vma=False,
    )
```

time: 305 us -> 89.4 us (0.29); the launches traced: 301 us -> 89.1 us
  waiting for transfers between devices: 219 us -> 0 us
  Pallas kernels: 0 us -> 82.2 us
  local copies, waits for them, and re-layouts: 30.4 us -> 6.28 us
  starting transfers between devices: 22.7 us -> 0 us
  between operations: 14.4 us -> 0.65 us
  matrix products: 6.93 us -> 0 us
  other arithmetic: 6.79 us -> 0 us
    ppermute x10 -> x0, waiting for transfers between devices: 112 us -> none  [partner(): return lax.ppermute(value, axis, pairs)]
    reduce_scatter x1 -> x0, waiting for transfers between devices: 107 us -> none  [per_device(): lax.psum_scatter(weight_acc * scale, 'rows', scatter_dimension=1, tiled=T...]
    pallas_call x0 -> x1, Pallas kernels: none -> 82.2 us  [per_device(): pl.pallas_call(body, out_shape=(jax.ShapeDtypeStruct((chan, tok), BF16),...]
    ppermute x10 -> x0, starting transfers between devices: 22.6 us -> none  [partner(): return lax.ppermute(value, axis, pairs)]
    rev x6 -> x0, local copies, waits for them, and re-layouts: 20.9 us -> none  [flip_axis(): return jnp.flip(h.reshape(shape), axis + 1).reshape(h.shape)]
    convert_element_type x10 -> x0, local copies, waits for them, and re-layouts: 7.08 us -> none  [the longest x5 3.55 us: combine(): theirs.astype(jnp.float32)]
    dot_general x4 -> x0, matrix products: 6.93 us -> none  [the longest x1 2.99 us: per_device(): jnp.dot(channel_weight, piece, preferred_element_type=jnp.float32)]
    convert_element_type x14 -> x0, other arithmetic: 6.64 us -> none  [the longest x7 5.29 us: combine(): (own * mine.astype(jnp.float32) + other * theirs.astype(jnp.float32)).ast...]
  transfers between devices with their start and end apart: 12 -> 0, of which waited for: 11 -> 0; matrix products, arithmetic and copies ran while one was open for 14% -> 0% of each run, Pallas kernels for 0% -> 0%
where the time goes in v1:
time: 89.4 us; the launch traced here: 89.1 us
  Pallas kernels  82.2 us (92%)
  local copies, waits for them, and re-layouts  6.28 us (7%)
    pallas_call x1, Pallas kernels, per_device(): pl.pallas_call(body, out_shape=(jax.ShapeDtypeStruct((chan, tok), BF16),...  82.2 us
    unnamed x11, local copies, waits for them, and re-layouts  5.58 us

profile of v1, /device:TPU:1, one launch (start us, length us, event | category | flops | bytes accessed | tf_op | source)
XLA Modules:
  0.0 89.1 jit_solution(358003611202493784)
XLA Ops:
  0.6 0.0 copy-start
  0.6 1.1 %copy-done = bf16[192,1536]{1,0:T(8,128)(2,1)S(1)} copy-done((bf16[192,1536]{1,0:T(8,128)(2,1)S(1)}, bf16[192,1536]{1,0:T(8,128)(2,1)}, u32[]{:S(2)}) %copy-start) | copy-done | bytes 589848
  1.7 0.0 copy-start.1
  1.7 1.0 %copy-done.1 = bf16[192,1024]{1,0:T(8,128)(2,1)S(1)} copy-done((bf16[192,1024]{1,0:T(8,128)(2,1)S(1)}, bf16[192,1024]{1,0:T(8,128)(2,1)}, u32[]{:S(2)}) %copy-start.1) | copy-done | bytes 393240
  2.7 0.0 copy-start.2
  2.7 1.0 %copy-done.2 = bf16[192,1024]{1,0:T(8,128)(2,1)S(1)} copy-done((bf16[192,1024]{1,0:T(8,128)(2,1)S(1)}, bf16[192,1024]{1,0:T(8,128)(2,1)}, u32[]{:S(2)}) %copy-start.2) | copy-done | bytes 393240
  3.7 0.0 copy-start.3
  3.7 0.9 %copy-done.3 = bf16[8,128,128]{2,1,0:T(8,128)(2,1)S(1)} copy-done((bf16[8,128,128]{2,1,0:T(8,128)(2,1)S(1)}, bf16[8,128,128]{2,1,0:T(8,128)(2,1)}, u32[]{:S(2)}) %copy-start.3) | copy-done | bytes 262168
  4.6 0.0 copy-start.4
  4.6 0.8 copy-done.4
  5.5 82.2 %mixer.1 = (bf16[192,1024]{1,0:T(8,128)(2,1)S(1)}, f32[192,48]{1,0:T(8,128)S(1)}) custom-call(bf16[192,1024]{1,0:T(8,128)(2,1)S(1)} %copy-done.1, bf16[192,1024]{1,0:T(8,128)(2,1)S(1)} %copy-done.2, bf16[8,128,128]{2,1,0:T(8,128)(2,1)S(1)} %copy-done.3, f32[2,8,1024]{2,1,0:T(8,128)S(1)} %copy-done.4, bf16[192,1536]{1,0:T(8,128)(2,1)S(1)} %copy-done), custom_call_target="tpu_custom_call" | custom-call | tf_op jit(solution)/shard_map/mixer/pallas_call | solution.py:383
  87.7 0.7 copy.7
  88.4 0.7 copy.9
Async XLA Ops:
  0.6 1.1 %copy-start = (bf16[192,1536]{1,0:T(8,128)(2,1)S(1)}, bf16[192,1536]{1,0:T(8,128)(2,1)}, u32[]{:S(2)}) copy-start(bf16[192,1536]{1,0:T(8,128)(2,1)} %w_hbm.1) | copy-start | bytes 1769476
  1.7 1.0 %copy-start.1 = (bf16[192,1024]{1,0:T(8,128)(2,1)S(1)}, bf16[192,1024]{1,0:T(8,128)(2,1)}, u32[]{:S(2)}) copy-start(bf16[192,1024]{1,0:T(8,128)(2,1)} %feat_hbm.1) | copy-start | bytes 1179652
  2.7 1.0 %copy-start.2 = (bf16[192,1024]{1,0:T(8,128)(2,1)S(1)}, bf16[192,1024]{1,0:T(8,128)(2,1)}, u32[]{:S(2)}) copy-start(bf16[192,1024]{1,0:T(8,128)(2,1)} %cot_hbm.1) | copy-start | bytes 1179652
  3.7 0.9 %copy-start.3 = (bf16[8,128,128]{2,1,0:T(8,128)(2,1)S(1)}, bf16[8,128,128]{2,1,0:T(8,128)(2,1)}, u32[]{:S(2)}) copy-start(bf16[8,128,128]{2,1,0:T(8,128)(2,1)} %blocks_hbm.1) | copy-start | bytes 786436
  4.6 0.8 copy-start.4

commit v2 on v1

v2 whole, which is shorter than its diff:
```python
import jax
import jax.numpy as jnp
from jax import lax
from jax.experimental import pallas as pl
from jax.experimental.pallas import tpu as pltpu
from jax.sharding import PartitionSpec as P

MESH = pl.DeviceIdType.MESH
F32 = jnp.float32
BF16 = jnp.bfloat16

NX, NZ, NC, NY = 4, 4, 2, 4
ROWS = NX * NZ * NC
NB = NZ * NC
CHS = 2 * NY
BLK = 128
LOCAL = 3
LEVELS = 8
CROSS = LEVELS - LOCAL
CHUNKS = NZ
TILE = 16


def gelu_parts(v):
    half = 0.5 * (1.0 + lax.erf(v * 0.7071067811865476))
    act = v * half
    slope = half + v * jnp.exp(-0.5 * v * v) * 0.3989422804014327
    return act, slope


def flip(v, dist):
    n = v.shape[0]
    h = v.reshape((n // (2 * dist), 2, dist) + v.shape[1:])
    h = jnp.concatenate([h[:, 1:], h[:, :1]], axis=1)
    return h.reshape(v.shape)


def span(start, size):
    return pl.ds(pl.multiple_of(start, size), size)


def body(
    feat_hbm, cot_hbm, blocks_hbm, tw_hbm, w_hbm,
    gf_ref, gw_ref,
    feat, blocks, tw, w, cot,
    twst, twz, twall, twb, twl, m0, act, slope,
    s1, r1, s2, s3, r3, s4, r4, bk,
    gst, rc, p1, rx, p2, rz,
    loc_sem, snd0, snd1, snd2, snd3, rcv0, rcv1, rcv2, rcv3, tw_send, tw_recv,
    cz_send, cz_recv, cy_send, cy_recv, g_send, g_recv,
):
    a2a_send, a2a_recv = (snd0, snd1, snd2, snd3), (rcv0, rcv1, rcv2, rcv3)
    row = lax.axis_index("rows")
    col = lax.axis_index("ch")
    x, zl, c = row // NB, (row // NC) % NZ, row % NC
    y, zh = col // 2, col % 2
    zc = row % NB
    up = {"ch": ((y + 1) % NY) * 2 + zh}
    down = {"ch": ((y + NY - 1) % NY) * 2 + zh}
    across = {"ch": y * 2 + (1 - zh)}
    chan, tok = feat.shape
    quarter = chan // NX
    tiles = quarter // TILE
    size = tok // CHUNKS
    group = gw_ref.shape[0]

    loads = [
        pltpu.make_async_copy(cot_hbm, cot.at[col], loc_sem.at[0]),
        pltpu.make_async_copy(tw_hbm, tw, loc_sem.at[1]),
        pltpu.make_async_copy(feat_hbm, feat, loc_sem.at[2]),
        pltpu.make_async_copy(blocks_hbm, blocks, loc_sem.at[3]),
        pltpu.make_async_copy(w_hbm, w, loc_sem.at[4]),
    ]
    for load in loads:
        load.start()

    bar = pltpu.get_barrier_semaphore()

    def greet(i, carry):
        pl.semaphore_signal(bar, inc=1, device_id={"rows": (row + i) % ROWS}, device_id_type=MESH)
        return carry

    lax.fori_loop(1, ROWS, greet, 0)
    for peer in (up, down, across):
        pl.semaphore_signal(bar, inc=1, device_id=peer, device_id_type=MESH)

    def local_fwd(t):
        for g in range(NB):
            lanes = slice(g * BLK, (g + 1) * BLK)
            left = jnp.concatenate(
                [feat[span(q * quarter + t * TILE, TILE), lanes] for q in range(NX)], axis=0
            )
            m0[g] = lax.dot_general(
                left, blocks[g], (((1,), (1,)), ((), ())), preferred_element_type=F32
            )

        def local_one(q, carry):
            v = m0[:, span(q * TILE, TILE), :].reshape(NB, 2, 8, BLK)
            for j in range(LOCAL):
                v = v * twl[0, j][:, None] + flip(v, 2**j) * twl[1, j][:, None]
            s1[q, :, span(t * TILE, TILE), :] = v.reshape(NB, TILE, BLK).astype(BF16)
            return carry

        lax.fori_loop(0, NX, local_one, 0)

    loads[1].wait()
    for b in range(NB):
        lanes = slice(b * BLK, (b + 1) * BLK)
        twst[b] = tw[:, :, lanes].reshape(2 * LEVELS, BLK).astype(BF16)

    loads[0].wait()
    pl.semaphore_wait(bar, ROWS - 1 + 3)

    def twz_send(i, carry):
        other = (zc + i) % NB
        pltpu.make_async_remote_copy(
            src_ref=twst.at[other], dst_ref=twz.at[zc],
            send_sem=tw_send.at[0], recv_sem=tw_recv.at[0],
            device_id={"rows": x * NB + other}, device_id_type=MESH,
        ).start()
        return carry

    lax.fori_loop(1, NB, twz_send, 0)
    pltpu.make_async_copy(twst.at[zc], twz.at[zc], tw_recv.at[0]).start()

    def exchange(step, t, src, dst, sem):
        part = span(t * TILE, TILE)

        def exch_one(i, carry):
            other = (row + i) % ROWS
            pltpu.make_async_remote_copy(
                src_ref=src.at[other // NB, other % NB, part], dst_ref=dst(row, part),
                send_sem=a2a_send[step].at[0], recv_sem=sem,
                device_id={"rows": other}, device_id_type=MESH,
            ).start()
            return carry

        lax.fori_loop(1, ROWS, exch_one, 0)
        pltpu.make_async_copy(src.at[x, zc, part], dst(row, part), sem).start()

    def slots(ref):
        return lambda r, part: ref.at[r // NB, r % NB, part]

    def arrived(step, t, ref):
        ref = ref.at[:, :, span(t * TILE, TILE)]
        pltpu.make_async_copy(ref, ref, a2a_recv[step].at[t]).wait()

    def chunk(k):
        return span(((zl + 1 + k) % NZ) * size, size)

    def cz(k):
        return pltpu.make_async_remote_copy(
            src_ref=cot.at[col, :, chunk(k)], dst_ref=cot.at[col, :, chunk(k)],
            send_sem=cz_send.at[k], recv_sem=cz_recv.at[k],
            device_id=across, device_id_type=MESH,
        )

    def cy(which, k, way, owner):
        return pltpu.make_async_remote_copy(
            src_ref=cot.at[owner, :, chunk(k)], dst_ref=cot.at[owner, :, chunk(k)],
            send_sem=cy_send.at[which, k, way], recv_sem=cy_recv.at[which, k, way],
            device_id=(up, down)[way], device_id_type=MESH,
        )

    sent = []

    def go(copy):
        copy.start()
        sent.append(copy)

    for k in range(CHUNKS):
        go(cz(k))
        for way in range(2):
            go(cy(0, k, way, col))

    for b in range(NB):
        lanes = slice(b * BLK, (b + 1) * BLK)
        for j in range(LOCAL):
            for s in range(2):
                twl[s, j, b] = jnp.broadcast_to(tw[s, j : j + 1, lanes], (8, BLK))

    loads[2].wait()
    loads[3].wait()
    for t in range(tiles):
        local_fwd(t)

    def relay(which, k):
        way = k % 2
        owner = ((y + NY - 1) % NY if way == 0 else (y + 1) % NY) * 2
        owner = owner + (zh if which == 0 else 1 - zh)
        cy(which, k, way, owner).wait_recv()
        go(cy(which + 1, k, way, owner))

    def far_send(k):
        cz(k).wait_recv()
        for way in range(2):
            go(cy(2, k, way, y * 2 + (1 - zh)))

    def spread(r, carry):
        u = twall[r // NB, r % NB].astype(F32)
        for j in range(CROSS):
            for s in range(2):
                at = s * LEVELS + LOCAL + j
                twb[s, j, r] = jnp.broadcast_to(u[at : at + 1, :], (8, BLK))
        return carry


    def cross_fwd(t):
        part = span(t * TILE, TILE)
        arrived(0, t, r1)
        v = r1[:, :, part, :].astype(F32).reshape(ROWS, 2, 8, BLK)
        for j in range(CROSS):
            v = v * twb[0, j][:, None] + flip(v, 2**j) * twb[1, j][:, None]
        slope[:, :, part, :] = v.reshape(NX, NB, TILE, BLK)

        def gelu_one(r, carry):
            a, s = gelu_parts(slope[r // NB, r % NB, part, :])
            s2[r // NB, r % NB, part, :] = a.astype(BF16)
            slope[r // NB, r % NB, part, :] = s
            return carry

        lax.fori_loop(0, ROWS, gelu_one, 0)
        exchange(
            1, t, s2,
            lambda r, _: act.at[span((r // NB) * quarter + t * TILE, TILE), span((r % NB) * BLK, BLK)],
            a2a_recv[1].at[0],
        )

    def project(k):
        way = k % 2
        for which in range(4):
            cy(which, k, way if which % 2 else 1 - way, col).wait_recv()
        piece = cot[:, :, chunk(k)].reshape(CHS * chan, size)
        back = jnp.dot(w[...], piece, preferred_element_type=F32).astype(BF16)
        first = ((zl + 1 + k) % NZ) * NC
        for q in range(NX):
            for j in range(NC):
                s3[q, first + j] = back[q * quarter : (q + 1) * quarter, j * BLK : (j + 1) * BLK]
        last = k == CHUNKS - 1
        for t in range(tiles):
            part = slice(t * TILE, (t + 1) * TILE)

            def a3_one(i, carry):
                at = (x * NC + c + i) % NB
                q, b = at // NC, first + at % NC
                pltpu.make_async_remote_copy(
                    src_ref=s3.at[q, b, part], dst_ref=r3.at[x, zc, part],
                    send_sem=a2a_send[2].at[0], recv_sem=a2a_recv[2].at[t],
                    device_id={"rows": q * NB + b}, device_id_type=MESH,
                ).start()
                return carry

            lax.fori_loop(1 if last else 0, NB, a3_one, 0)
            if last:
                pltpu.make_async_copy(
                    s3.at[x, zc, part], r3.at[x, zc, part], a2a_recv[2].at[t]
                ).start()

    relay(0, 0)
    pltpu.make_async_copy(twz, twz, tw_recv.at[0]).wait()

    def twx_send(i, carry):
        other = (x + i) % NX
        pltpu.make_async_remote_copy(
            src_ref=twz, dst_ref=twall.at[x],
            send_sem=tw_send.at[1], recv_sem=tw_recv.at[1],
            device_id={"rows": other * NB + zc}, device_id_type=MESH,
        ).start()
        return carry

    lax.fori_loop(1, NX, twx_send, 0)
    pltpu.make_async_copy(twz, twall.at[x], tw_recv.at[1]).start()

    relay(0, 1)
    far_send(0)
    for t in range(tiles):
        exchange(0, t, s1, slots(r1), a2a_recv[0].at[t])
    relay(0, 2)
    pltpu.make_async_copy(twall, twall, tw_recv.at[1]).wait()
    lax.fori_loop(0, ROWS, spread, 0)
    far_send(1)
    relay(2, 0)
    relay(0, 3)
    far_send(2)
    relay(2, 1)
    cross_fwd(0)
    far_send(3)
    relay(2, 2)
    cross_fwd(1)
    loads[4].wait()
    relay(2, 3)
    cross_fwd(2)
    project(0)
    project(1)
    project(2)
    project(3)

    pltpu.make_async_copy(act, act, a2a_recv[1].at[0]).wait()

    def weight(h, carry):
        g = lax.dot_general(
            cot[h], act[...], (((1,), (1,)), ((), ())), preferred_element_type=F32
        ).astype(BF16)
        for i in range(4):
            gst[i % 2, h // 2, (h % 2) * 2 + i // 2] = g[i * group : (i + 1) * group]
        return carry

    lax.fori_loop(0, CHS, weight, 0)
    g_core = pltpu.make_async_remote_copy(
        src_ref=gst.at[1 - c], dst_ref=rc, send_sem=g_send.at[0], recv_sem=g_recv.at[0],
        device_id={"rows": row + 1 - 2 * c}, device_id_type=MESH,
    )
    go(g_core)

    def cross_bwd(t):
        part = span(t * TILE, TILE)
        arrived(2, t, r3)
        v = r3[:, :, part, :].astype(F32) * slope[:, :, part, :]
        v = v.reshape(ROWS, 2, 8, BLK)
        for j in reversed(range(CROSS)):
            v = v * twb[0, j][:, None] + flip(v * twb[1, j][:, None], 2**j)
        s4[:, :, part, :] = v.reshape(NX, NB, TILE, BLK).astype(BF16)
        exchange(3, t, s4, slots(r4), a2a_recv[3].at[t])

    for t in range(tiles):
        cross_bwd(t)

    g_core.wait_recv()
    for i in range(NX):
        p1[i] = (gst[c, i].astype(F32) + rc[i].astype(F32)).astype(BF16)

    def gx(i, carry):
        other = (x + i) % NX
        pltpu.make_async_remote_copy(
            src_ref=p1.at[other], dst_ref=rx.at[x], send_sem=g_send.at[1], recv_sem=g_recv.at[1],
            device_id={"rows": other * NB + zc}, device_id_type=MESH,
        ).start()
        return carry

    lax.fori_loop(1, NX, gx, 0)
    pltpu.make_async_copy(p1.at[x], rx.at[x], g_recv.at[1]).start()

    def local_bwd(t):
        arrived(3, t, r4)

        def bwd_one(q, carry):
            v = r4[q, :, span(t * TILE, TILE), :].astype(F32).reshape(NB, 2, 8, BLK)
            for j in reversed(range(LOCAL)):
                v = v * twl[0, j][:, None] + flip(v * twl[1, j][:, None], 2**j)
            bk[:, span(q * TILE, TILE), :] = v.reshape(NB, TILE, BLK).astype(BF16)
            return carry

        lax.fori_loop(0, NX, bwd_one, 0)
        for g in range(NB):
            out = jnp.dot(bk[g], blocks[g], preferred_element_type=F32).astype(BF16)
            for q in range(NX):
                gf_ref[span(q * quarter + t * TILE, TILE), g * BLK : (g + 1) * BLK] = out[
                    q * TILE : (q + 1) * TILE
                ]

    local_bwd(0)
    pltpu.make_async_copy(rx, rx, g_recv.at[1]).wait()
    for i in range(NZ):
        total = rx[0, i].astype(F32)
        for j in range(1, NX):
            total = total + rx[j, i].astype(F32)
        p2[i] = total.astype(BF16)

    def gz(i, carry):
        other = (zl + i) % NZ
        pltpu.make_async_remote_copy(
            src_ref=p2.at[other], dst_ref=rz.at[zl], send_sem=g_send.at[2], recv_sem=g_recv.at[2],
            device_id={"rows": x * NB + other * NC + c}, device_id_type=MESH,
        ).start()
        return carry

    lax.fori_loop(1, NZ, gz, 0)
    pltpu.make_async_copy(p2.at[zl], rz.at[zl], g_recv.at[2]).start()

    for t in range(1, tiles):
        local_bwd(t)

    pltpu.make_async_copy(rz, rz, g_recv.at[2]).wait()
    total = rz[0].astype(F32)
    for j in range(1, NZ):
        total = total + rz[j].astype(F32)
    gw_ref[...] = total * (1.0 / (tok * ROWS) ** 0.5)

    for step, src in enumerate((s1, s2, s3, s4)):
        for part in (src.at[0:3], src.at[3, 0:7]):
            pltpu.make_async_copy(part, part, a2a_send[step].at[0]).wait()
    pltpu.make_async_copy(twst.at[0:7], twst.at[0:7], tw_send.at[0]).wait()
    pltpu.make_async_copy(twall.at[0:3], twall.at[0:3], tw_send.at[1]).wait()
    for copy in sent:
        copy.wait_send()
    pltpu.make_async_copy(p1.at[0:3], p1.at[0:3], g_send.at[1]).wait()
    pltpu.make_async_copy(p2.at[0:3], p2.at[0:3], g_send.at[2]).wait()


def per_device(features, cotangent, blocks, twiddles, channel_weight):
    chan, tok = features.shape
    quarter = chan // NX
    group = channel_weight.shape[1] // ROWS
    piece = (NX, NB, quarter, BLK)
    vm = pltpu.VMEM
    dma = pltpu.SemaphoreType.DMA
    scratch = [
        vm((chan, tok), BF16), vm(blocks.shape, BF16), vm(twiddles.shape, F32),
        vm(channel_weight.shape, BF16), vm((CHS, chan, tok), BF16),
        vm((NB, 2 * LEVELS, BLK), BF16), vm((NB, 2 * LEVELS, BLK), BF16),
        vm((NX, NB, 2 * LEVELS, BLK), BF16),
        vm((2, CROSS, ROWS, 8, BLK), F32), vm((2, LOCAL, NB, 8, BLK), F32),
        vm((NB, NX * TILE, BLK), F32), vm((chan, tok), BF16), vm(piece, F32),
        *[vm(piece, BF16)] * 7, vm((NB, NX * TILE, BLK), BF16),
        vm((NC, NX, NZ, group, chan), BF16), vm((NX, NZ, group, chan), BF16),
        vm((NX, NZ, group, chan), BF16), vm((NX, NZ, group, chan), BF16),
        vm((NZ, group, chan), BF16), vm((NZ, group, chan), BF16),
        dma((5,)), *[dma((1,))] * 4, *[dma((3,))] * 4, dma((2,)), dma((2,)),
        dma((CHUNKS,)), dma((CHUNKS,)), dma((4, CHUNKS, 2)), dma((4, CHUNKS, 2)),
        dma((3,)), dma((3,)),
    ]
    grad_features, grad_weight = pl.pallas_call(
        body,
        out_shape=(
            jax.ShapeDtypeStruct((chan, tok), BF16),
            jax.ShapeDtypeStruct((group, chan), F32),
        ),
        in_specs=[pl.BlockSpec(memory_space=pltpu.HBM)] * 5,
        out_specs=(pl.BlockSpec(memory_space=pltpu.VMEM),) * 2,
        scratch_shapes=scratch,
        name="mixer",
        compiler_params=pltpu.CompilerParams(
            collective_id=0, has_side_effects=True, vmem_limit_bytes=60 << 20
        ),
    )(features, cotangent, blocks, twiddles, channel_weight)
    return grad_features, grad_weight.T


def solution(mesh):
    return jax.shard_map(
        per_device,
        mesh=mesh,
        in_specs=(
            P("ch", "rows"),
            P("ch", "rows"),
            P("rows", None, None),
            P(None, None, "rows"),
            P("ch", None),
        ),
        out_specs=(P("ch", "rows"), P("ch", "rows")),
        check_vma=False,
    )
```

time: 89.4 us -> 75.6 us (0.85)
  Pallas kernels: 82.2 us -> 72.4 us
  local copies, waits for them, and re-layouts: 6.28 us -> 2.4 us
    pallas_call x1, Pallas kernels: 82.2 us -> 72.4 us  [per_device(): pl.pallas_call(body, out_shape=(jax.ShapeDtypeStruct((chan, tok), BF16),...]
    unnamed x11 -> x4, local copies, waits for them, and re-layouts: 5.58 us -> 2.4 us
where the time goes in v2:
time: 75.6 us; the launch traced here: 75.5 us
  Pallas kernels  72.4 us (96%)
  local copies, waits for them, and re-layouts  2.4 us (3%)
    pallas_call x1, Pallas kernels, per_device(): pl.pallas_call(body, out_shape=(jax.ShapeDtypeStruct((chan, tok), BF16),...  72.4 us
    unnamed x4, local copies, waits for them, and re-layouts  2.4 us

profile of v2, /device:TPU:1, one launch (start us, length us, event | category | flops | bytes accessed | tf_op | source)
XLA Modules:
  0.0 75.5 jit_solution(16494085658588254476)
XLA Ops:
  0.6 72.4 %mixer.1 = (bf16[192,1024]{1,0:T(8,128)(2,1)}, f32[48,192]{1,0:T(8,128)}) custom-call(bf16[192,1024]{1,0:T(8,128)(2,1)} %feat_hbm.1, bf16[192,1024]{1,0:T(8,128)(2,1)} %cot_hbm.1, bf16[8,128,128]{2,1,0:T(8,128)(2,1)} %blocks_hbm.1, f32[2,8,1024]{2,1,0:T(8,128)} %tw_hbm.1, bf16[192,1536]{1,0:T(8,128)(2,1)} %w_hbm.1), custom_call_target="tpu_custom_call" | custom-call | tf_op jit(solution)/shard_map/mixer/pallas_call | solution.py:422
  73.1 0.0 copy-start
  73.1 1.8 %copy.9 = bf16[192,1024]{1,0:T(8,128)(2,1)} copy(bf16[192,1024]{1,0:T(8,128)(2,1)} %get-tuple-element.8) | data formatting | bytes 786432
  74.9 0.0 copy-done
  74.9 0.6 copy.10
Async XLA Ops:
  73.1 1.8 %copy-start = (f32[48,192]{1,0:T(8,128)S(1)}, f32[48,192]{1,0:T(8,128)}, u32[]{:S(2)}) copy-start(f32[48,192]{1,0:T(8,128)} %get-tuple-element.5) | copy-start | bytes 110596

commit v3 on v2

--- a/solution.py
+++ b/solution.py
@@ -18,6 +18,7 @@
 LEVELS = 8
 CROSS = LEVELS - LOCAL
 CHUNKS = NZ
+PARTS = 2
 TILE = 16
 
 
@@ -41,11 +42,11 @@
 
 def body(
     feat_hbm, cot_hbm, blocks_hbm, tw_hbm, w_hbm,
-    gf_ref, gw_ref,
+    gf_hbm, gw_hbm,
     feat, blocks, tw, w, cot,
     twst, twz, twall, twb, twl, m0, act, slope,
     s1, r1, s2, s3, r3, s4, r4, bk,
-    gst, rc, p1, rx, p2, rz,
+    gst, rc, p1, rx, p2, rz, gf_ref, gw_ref, out_sem,
     loc_sem, snd0, snd1, snd2, snd3, rcv0, rcv1, rcv2, rcv3, tw_send, tw_recv,
     cz_send, cz_recv, cy_send, cy_recv, g_send, g_recv,
 ):
@@ -295,23 +296,6 @@
     project(2)
     project(3)
 
-    pltpu.make_async_copy(act, act, a2a_recv[1].at[0]).wait()
-
-    def weight(h, carry):
-        g = lax.dot_general(
-            cot[h], act[...], (((1,), (1,)), ((), ())), preferred_element_type=F32
-        ).astype(BF16)
-        for i in range(4):
-            gst[i % 2, h // 2, (h % 2) * 2 + i // 2] = g[i * group : (i + 1) * group]
-        return carry
-
-    lax.fori_loop(0, CHS, weight, 0)
-    g_core = pltpu.make_async_remote_copy(
-        src_ref=gst.at[1 - c], dst_ref=rc, send_sem=g_send.at[0], recv_sem=g_recv.at[0],
-        device_id={"rows": row + 1 - 2 * c}, device_id_type=MESH,
-    )
-    go(g_core)
-
     def cross_bwd(t):
         part = span(t * TILE, TILE)
         arrived(2, t, r3)
@@ -322,23 +306,7 @@
         s4[:, :, part, :] = v.reshape(NX, NB, TILE, BLK).astype(BF16)
         exchange(3, t, s4, slots(r4), a2a_recv[3].at[t])
 
-    for t in range(tiles):
-        cross_bwd(t)
-
-    g_core.wait_recv()
-    for i in range(NX):
-        p1[i] = (gst[c, i].astype(F32) + rc[i].astype(F32)).astype(BF16)
-
-    def gx(i, carry):
-        other = (x + i) % NX
-        pltpu.make_async_remote_copy(
-            src_ref=p1.at[other], dst_ref=rx.at[x], send_sem=g_send.at[1], recv_sem=g_recv.at[1],
-            device_id={"rows": other * NB + zc}, device_id_type=MESH,
-        ).start()
-        return carry
-
-    lax.fori_loop(1, NX, gx, 0)
-    pltpu.make_async_copy(p1.at[x], rx.at[x], g_recv.at[1]).start()
+    written = []
 
     def local_bwd(t):
         arrived(3, t, r4)
@@ -357,8 +325,50 @@
                 gf_ref[span(q * quarter + t * TILE, TILE), g * BLK : (g + 1) * BLK] = out[
                     q * TILE : (q + 1) * TILE
                 ]
-
-    local_bwd(0)
+        for q in range(NX):
+            part = span(q * quarter + t * TILE, TILE)
+            copy = pltpu.make_async_copy(gf_ref.at[part], gf_hbm.at[part], out_sem.at[t, q])
+            copy.start()
+            written.append(copy)
+
+    pltpu.make_async_copy(act, act, a2a_recv[1].at[0]).wait()
+
+    def weight(h, carry):
+        g = lax.dot_general(
+            cot[h], act[...], (((1,), (1,)), ((), ())), preferred_element_type=F32
+        ).astype(BF16)
+        for i in range(4):
+            gst[i % 2, h // 2, (h % 2) * 2 + i // 2] = g[i * group : (i + 1) * group]
+        return carry
+
+    lax.fori_loop(0, CHS, weight, 0)
+    g_core = pltpu.make_async_remote_copy(
+        src_ref=gst.at[1 - c], dst_ref=rc, send_sem=g_send.at[0], recv_sem=g_recv.at[0],
+        device_id={"rows": row + 1 - 2 * c}, device_id_type=MESH,
+    )
+    go(g_core)
+
+    cross_bwd(0)
+
+    g_core.wait_recv()
+    for i in range(NX):
+        p1[i] = (gst[c, i].astype(F32) + rc[i].astype(F32)).astype(BF16)
+
+    def gx(i, carry):
+        other = (x + i) % NX
+        pltpu.make_async_remote_copy(
+            src_ref=p1.at[other], dst_ref=rx.at[x], send_sem=g_send.at[1], recv_sem=g_recv.at[1],
+            device_id={"rows": other * NB + zc}, device_id_type=MESH,
+        ).start()
+        return carry
+
+    lax.fori_loop(1, NX, gx, 0)
+    pltpu.make_async_copy(p1.at[x], rx.at[x], g_recv.at[1]).start()
+
+    cross_bwd(1)
+
+    cross_bwd(2)
+
     pltpu.make_async_copy(rx, rx, g_recv.at[1]).wait()
     for i in range(NZ):
         total = rx[0, i].astype(F32)
@@ -377,7 +387,7 @@
     lax.fori_loop(1, NZ, gz, 0)
     pltpu.make_async_copy(p2.at[zl], rz.at[zl], g_recv.at[2]).start()
 
-    for t in range(1, tiles):
+    for t in range(tiles):
         local_bwd(t)
 
     pltpu.make_async_copy(rz, rz, g_recv.at[2]).wait()
@@ -385,6 +395,11 @@
     for j in range(1, NZ):
         total = total + rz[j].astype(F32)
     gw_ref[...] = total * (1.0 / (tok * ROWS) ** 0.5)
+    copy = pltpu.make_async_copy(gw_ref, gw_hbm, loc_sem.at[5])
+    copy.start()
+    written.append(copy)
+    for copy in written:
+        copy.wait()
 
     for step, src in enumerate((s1, s2, s3, s4)):
         for part in (src.at[0:3], src.at[3, 0:7]):
@@ -395,6 +410,11 @@
         copy.wait_send()
     pltpu.make_async_copy(p1.at[0:3], p1.at[0:3], g_send.at[1]).wait()
     pltpu.make_async_copy(p2.at[0:3], p2.at[0:3], g_send.at[2]).wait()
+
+
+def hand_over(gf_in, gw_in, gf_out, gw_out):
+    gf_out[...] = gf_in[...]
+    gw_out[...] = gw_in[...]
 
 
 def per_device(features, cotangent, blocks, twiddles, channel_weight):
@@ -415,7 +435,8 @@
         vm((NC, NX, NZ, group, chan), BF16), vm((NX, NZ, group, chan), BF16),
         vm((NX, NZ, group, chan), BF16), vm((NX, NZ, group, chan), BF16),
         vm((NZ, group, chan), BF16), vm((NZ, group, chan), BF16),
-        dma((5,)), *[dma((1,))] * 4, *[dma((3,))] * 4, dma((2,)), dma((2,)),
+        vm((chan, tok), BF16), vm((group, chan), F32), dma((3, NX)),
+        dma((6,)), *[dma((1,))] * 4, *[dma((3,))] * 4, dma((2,)), dma((2,)),
         dma((CHUNKS,)), dma((CHUNKS,)), dma((4, CHUNKS, 2)), dma((4, CHUNKS, 2)),
         dma((3,)), dma((3,)),
     ]
@@ -426,13 +447,29 @@
             jax.ShapeDtypeStruct((group, chan), F32),
         ),
         in_specs=[pl.BlockSpec(memory_space=pltpu.HBM)] * 5,
-        out_specs=(pl.BlockSpec(memory_space=pltpu.VMEM),) * 2,
+        out_specs=(pl.BlockSpec(memory_space=pl.ANY),) * 2,
         scratch_shapes=scratch,
         name="mixer",
         compiler_params=pltpu.CompilerParams(
             collective_id=0, has_side_effects=True, vmem_limit_bytes=60 << 20
         ),
     )(features, cotangent, blocks, twiddles, channel_weight)
+    steps = [
+        pl.BlockSpec((chan // PARTS, tok), lambda i: (i, 0)),
+        pl.BlockSpec((group, chan), lambda i: (0, 0)),
+    ]
+    grad_features, grad_weight = pl.pallas_call(
+        hand_over,
+        out_shape=(
+            jax.ShapeDtypeStruct((chan, tok), BF16),
+            jax.ShapeDtypeStruct((group, chan), F32),
+        ),
+        grid=(PARTS,),
+        in_specs=steps,
+        out_specs=steps,
+        name="hand_over",
+        compiler_params=pltpu.CompilerParams(vmem_limit_bytes=60 << 20),
+    )(grad_features, grad_weight)
     return grad_features, grad_weight.T
 
 

time: 75.6 us -> 74.3 us (0.983)
  local copies, waits for them, and re-layouts: 2.4 us -> 0 us
  Pallas kernels: 72.4 us -> 73.5 us
    unnamed x4 -> x0, local copies, waits for them, and re-layouts: 2.4 us -> none
    pallas_call x0 -> x1, Pallas kernels: none -> 1.76 us  [per_device(): pl.pallas_call(hand_over, out_shape=(jax.ShapeDtypeStruct((chan, tok), BF...]
where the time goes in v3:
time: 74.3 us; the launch traced here: 74.1 us
  Pallas kernels  73.5 us (99%)
    pallas_call x1, Pallas kernels, per_device(): pl.pallas_call(body, out_shape=(jax.ShapeDtypeStruct((chan, tok), BF16),...  71.7 us
    pallas_call x1, Pallas kernels, per_device(): pl.pallas_call(hand_over, out_shape=(jax.ShapeDtypeStruct((chan, tok), BF...  1.76 us

profile of v3, /device:TPU:1, one launch (start us, length us, event | category | flops | bytes accessed | tf_op | source)
XLA Modules:
  0.0 74.1 jit_solution(2159889237917561761)
XLA Ops:
  0.6 71.7 %mixer.1 = (bf16[192,1024]{1,0:T(8,128)(2,1)}, f32[48,192]{1,0:T(8,128)}) custom-call(bf16[192,1024]{1,0:T(8,128)(2,1)} %feat_hbm.1, bf16[192,1024]{1,0:T(8,128)(2,1)} %cot_hbm.1, bf16[8,128,128]{2,1,0:T(8,128)(2,1)} %blocks_hbm.1, f32[2,8,1024]{2,1,0:T(8,128)} %tw_hbm.1, bf16[192,1536]{1,0:T(8,128)(2,1)} %w_hbm.1), custom_call_target="tpu_custom_call" | custom-call | tf_op jit(solution)/shard_map/mixer/pallas_call | solution.py:443
  72.4 1.8 %hand_over.1 = (bf16[192,1024]{1,0:T(8,128)(2,1)}, f32[48,192]{1,0:T(8,128)}) custom-call(bf16[192,1024]{1,0:T(8,128)(2,1)} %get-tuple-element.6.gf_in, f32[48,192]{1,0:T(8,128)} %get-tuple-element.7.gw_in), custom_call_target="tpu_custom_call" | custom-call | tf_op jit(solution)/shard_map/hand_over/pallas_call | solution.py:461

commit v4 on v3

--- a/solution.py
+++ b/solution.py
@@ -341,16 +341,17 @@
             gst[i % 2, h // 2, (h % 2) * 2 + i // 2] = g[i * group : (i + 1) * group]
         return carry
 
-    lax.fori_loop(0, CHS, weight, 0)
-    g_core = pltpu.make_async_remote_copy(
-        src_ref=gst.at[1 - c], dst_ref=rc, send_sem=g_send.at[0], recv_sem=g_recv.at[0],
-        device_id={"rows": row + 1 - 2 * c}, device_id_type=MESH,
-    )
-    go(g_core)
+    for i in range(NX):
+        lax.fori_loop(2 * i, 2 * i + 2, weight, 0)
+        pltpu.make_async_remote_copy(
+            src_ref=gst.at[1 - c, i], dst_ref=rc.at[i],
+            send_sem=g_send.at[0], recv_sem=g_recv.at[0],
+            device_id={"rows": row + 1 - 2 * c}, device_id_type=MESH,
+        ).start()
 
     cross_bwd(0)
 
-    g_core.wait_recv()
+    pltpu.make_async_copy(rc, rc, g_recv.at[0]).wait()
     for i in range(NX):
         p1[i] = (gst[c, i].astype(F32) + rc[i].astype(F32)).astype(BF16)
 
@@ -408,6 +409,7 @@
     pltpu.make_async_copy(twall.at[0:3], twall.at[0:3], tw_send.at[1]).wait()
     for copy in sent:
         copy.wait_send()
+    pltpu.make_async_copy(rc, rc, g_send.at[0]).wait()
     pltpu.make_async_copy(p1.at[0:3], p1.at[0:3], g_send.at[1]).wait()
     pltpu.make_async_copy(p2.at[0:3], p2.at[0:3], g_send.at[2]).wait()
 

time: 74.3 us -> 73.7 us (level)
  no operation moved by 1% of the time
where the time goes in v4:
time: 73.7 us; the launch traced here: 73.5 us
  Pallas kernels  72.8 us (99%)
    pallas_call x1, Pallas kernels, per_device(): pl.pallas_call(body, out_shape=(jax.ShapeDtypeStruct((chan, tok), BF16),...  71.1 us
    pallas_call x1, Pallas kernels, per_device(): pl.pallas_call(hand_over, out_shape=(jax.ShapeDtypeStruct((chan, tok), BF...  1.76 us

profile of v4, /device:TPU:1, one launch (start us, length us, event | category | flops | bytes accessed | tf_op | source)
XLA Modules:
  0.0 73.5 jit_solution(6818038321831511498)
XLA Ops:
  0.6 71.1 %mixer.1 = (bf16[192,1024]{1,0:T(8,128)(2,1)}, f32[48,192]{1,0:T(8,128)}) custom-call(bf16[192,1024]{1,0:T(8,128)(2,1)} %feat_hbm.1, bf16[192,1024]{1,0:T(8,128)(2,1)} %cot_hbm.1, bf16[8,128,128]{2,1,0:T(8,128)(2,1)} %blocks_hbm.1, f32[2,8,1024]{2,1,0:T(8,128)} %tw_hbm.1, bf16[192,1536]{1,0:T(8,128)(2,1)} %w_hbm.1), custom_call_target="tpu_custom_call" | custom-call | tf_op jit(solution)/shard_map/mixer/pallas_call | solution.py:445
  71.7 1.8 %hand_over.1 = (bf16[192,1024]{1,0:T(8,128)(2,1)}, f32[48,192]{1,0:T(8,128)}) custom-call(bf16[192,1024]{1,0:T(8,128)(2,1)} %get-tuple-element.6.gf_in, f32[48,192]{1,0:T(8,128)} %get-tuple-element.7.gw_in), custom_call_target="tpu_custom_call" | custom-call | tf_op jit(solution)/shard_map/hand_over/pallas_call | solution.py:463

commit v5 on v4

--- a/solution.py
+++ b/solution.py
@@ -214,13 +214,14 @@
             v = v * twb[0, j][:, None] + flip(v, 2**j) * twb[1, j][:, None]
         slope[:, :, part, :] = v.reshape(NX, NB, TILE, BLK)
 
-        def gelu_one(r, carry):
-            a, s = gelu_parts(slope[r // NB, r % NB, part, :])
-            s2[r // NB, r % NB, part, :] = a.astype(BF16)
-            slope[r // NB, r % NB, part, :] = s
+        def gelu_one(i, carry):
+            q, b = i // 2, (i % 2) * 4
+            a, slant = gelu_parts(slope[q, pl.ds(b, 4), part, :])
+            s2[q, pl.ds(b, 4), part, :] = a.astype(BF16)
+            slope[q, pl.ds(b, 4), part, :] = slant
             return carry
 
-        lax.fori_loop(0, ROWS, gelu_one, 0)
+        lax.fori_loop(0, NX * 2, gelu_one, 0)
         exchange(
             1, t, s2,
             lambda r, _: act.at[span((r // NB) * quarter + t * TILE, TILE), span((r % NB) * BLK, BLK)],

time: 73.7 us -> 73.7 us (level)
  no operation moved by 1% of the time
where the time goes in v5:
time: 73.7 us; the launch traced here: 73.2 us
  Pallas kernels  72.6 us (99%)
    pallas_call x1, Pallas kernels, per_device(): pl.pallas_call(body, out_shape=(jax.ShapeDtypeStruct((chan, tok), BF16),...  70.8 us
    pallas_call x1, Pallas kernels, per_device(): pl.pallas_call(hand_over, out_shape=(jax.ShapeDtypeStruct((chan, tok), BF...  1.76 us

profile of v5, /device:TPU:1, one launch (start us, length us, event | category | flops | bytes accessed | tf_op | source)
XLA Modules:
  0.0 73.2 jit_solution(13693559631332123552)
XLA Ops:
  0.6 70.8 %mixer.1 = (bf16[192,1024]{1,0:T(8,128)(2,1)}, f32[48,192]{1,0:T(8,128)}) custom-call(bf16[192,1024]{1,0:T(8,128)(2,1)} %feat_hbm.1, bf16[192,1024]{1,0:T(8,128)(2,1)} %cot_hbm.1, bf16[8,128,128]{2,1,0:T(8,128)(2,1)} %blocks_hbm.1, f32[2,8,1024]{2,1,0:T(8,128)} %tw_hbm.1, bf16[192,1536]{1,0:T(8,128)(2,1)} %w_hbm.1), custom_call_target="tpu_custom_call" | custom-call | tf_op jit(solution)/shard_map/mixer/pallas_call | solution.py:446
  71.5 1.8 %hand_over.1 = (bf16[192,1024]{1,0:T(8,128)(2,1)}, f32[48,192]{1,0:T(8,128)}) custom-call(bf16[192,1024]{1,0:T(8,128)(2,1)} %get-tuple-element.6.gf_in, f32[48,192]{1,0:T(8,128)} %get-tuple-element.7.gw_in), custom_call_target="tpu_custom_call" | custom-call | tf_op jit(solution)/shard_map/hand_over/pallas_call | solution.py:464
